TPU v7x, 32 devices: a whole 2x2x4 slice. The times are simulated.
32 devices in a mesh: wide: 8 (over y, x, core), narrow: 4 (over z).
Axes of the slice: x: 2, y: 2, z: 4, core: 2. Of those that a mesh axis runs over, the one named last changes fastest.
Arguments:
- raw_samples: bfloat16 [256, 8, 16384], P(('wide', 'narrow')), as said below
- filter_taps: float32 [64], replicated, may hold values from -0.75 to 0.75
- tile_pairs: int32 [16, 2], replicated, may hold values from 0 to 31, as said below
- tile_owners: int32 [16], replicated, may hold values from 0 to 3, as said below
Outputs:
- correlation_stacks: float32 [32, 64, 512], P('narrow', 'wide')
Inputs may be any that keep to these rules, and one draw needn't show every extreme that they name: `raw_samples`: noise samples, scaled per channel and per window. `tile_pairs`: each row is (source block, receiver block), and the two blocks differ. `tile_owners`: each owner has at most 8 tiles, and some owner has exactly 8.
All inputs are finite; a program needn't handle non-finite values.
Results may differ from a plain program's by a relative error of at most 0.0074.
Values may be sent and summed in bfloat16 or wider, within the bound.
A program may use at most 128 MiB of HBM per device.

v0:
```python
import math

import jax
import jax.numpy as jnp
from jax import lax
from jax.sharding import PartitionSpec as P

NFFT = 4096
DECIM = 4
NBINS = 1024
SMOOTH = 63
LAGS = 512
BLK = 8
SLOTS = 8


water_level = 0.2
epsilon = 1e-06


def fir_tables(filter_taps, block_size):
    in_rows = jnp.arange(DECIM * block_size, dtype=jnp.int32)[:, None]
    out_cols = jnp.arange(block_size, dtype=jnp.int32)[None, :]
    this_index = DECIM * out_cols + DECIM - 1 - in_rows
    last_index = this_index + DECIM * block_size
    tap_count = filter_taps.shape[0]

    def taps_at(tap_index):
        inside = (tap_index >= 0) & (tap_index < tap_count)
        values = jnp.take(filter_taps, jnp.clip(tap_index, 0, tap_count - 1))
        return jnp.where(inside, values, jnp.zeros_like(values)).astype(jnp.bfloat16)

    return (taps_at(this_index), taps_at(last_index))


def decimate(samples, filter_taps):
    row_count, row_length = samples.shape
    block_size = min(128, row_length // DECIM)
    this_table, last_table = fir_tables(filter_taps, block_size)
    segments = samples.reshape(-1, DECIM * block_size)
    current = jnp.dot(segments, this_table, preferred_element_type=jnp.float32).reshape(
        row_count, -1, block_size
    )
    spilled = jnp.dot(segments, last_table, preferred_element_type=jnp.float32).reshape(
        row_count, -1, block_size
    )
    spilled = jnp.pad(spilled[:, :-1], ((0, 0), (1, 0), (0, 0)))
    return (current + spilled).reshape(row_count, -1).astype(jnp.bfloat16)


def dft_table(point_count, bin_count):
    sample_index = jnp.arange(point_count, dtype=jnp.int32)[:, None]
    frequency = 1 + jnp.arange(bin_count, dtype=jnp.int32)[None, :]
    angle = (sample_index * frequency % point_count).astype(jnp.float32) * (
        2.0 * math.pi / point_count
    )
    return jnp.concatenate([jnp.cos(angle), -jnp.sin(angle)], axis=1).astype(jnp.bfloat16)


def lag_table(point_count, bin_count, lag_count, window_count):
    frequency = 1 + jnp.arange(bin_count, dtype=jnp.int32)[:, None]
    shifted = jnp.arange(lag_count, dtype=jnp.int32)[None, :] - lag_count // 2 + point_count
    angle = (frequency * shifted % point_count).astype(jnp.float32) * (2.0 * math.pi / point_count)
    weight = 1.0 / math.sqrt(window_count * bin_count)
    return jnp.concatenate([jnp.cos(angle) * weight, -jnp.sin(angle) * weight], axis=0)


def smoother(bin_count, span_width):
    bin_index = jnp.arange(bin_count, dtype=jnp.int32)
    nearby = (jnp.abs(bin_index[:, None] - bin_index[None, :]) <= (span_width - 1) // 2).astype(
        jnp.float32
    )
    return nearby / jnp.sum(nearby, axis=0, keepdims=True)


def whiten(decimated):
    spectrum = jnp.dot(
        decimated, dft_table(decimated.shape[1], NBINS), preferred_element_type=jnp.float32
    )
    real_part = spectrum[:, :NBINS]
    imag_part = spectrum[:, NBINS:]
    magnitude = jnp.sqrt(real_part * real_part + imag_part * imag_part)
    smooth = jnp.dot(magnitude, smoother(NBINS, SMOOTH), precision=lax.Precision.HIGHEST)
    floor_level = water_level * jnp.mean(smooth, axis=1, keepdims=True) + epsilon
    factor = 1.0 / (smooth + floor_level)
    return (spectrum * jnp.concatenate([factor, factor], axis=1)).astype(jnp.bfloat16)


def block_start(block_index, chan_dev, wide_count, narrow_count):
    first_channel = block_index * BLK
    shard_index = first_channel // chan_dev
    return (
        shard_index % narrow_count * wide_count + shard_index // narrow_count
    ) * chan_dev + first_channel % chan_dev


def gather_rows(spectra, starts):

    def one_block(start_row):
        return lax.dynamic_slice_in_dim(spectra, start_row, BLK, 0)

    return jax.vmap(one_block)(starts)


def slot_cross(source, target, live_slots):
    highest = lax.Precision.HIGHEST
    src_real = source[..., :NBINS]
    src_imag = source[..., NBINS:]
    dst_real = target[..., :NBINS]
    dst_imag = target[..., NBINS:]
    real_sum = jnp.einsum("siwf,sjwf->ijsf", src_real, dst_real, precision=highest) + jnp.einsum(
        "siwf,sjwf->ijsf", src_imag, dst_imag, precision=highest
    )
    imag_sum = jnp.einsum("siwf,sjwf->ijsf", src_real, dst_imag, precision=highest) - jnp.einsum(
        "siwf,sjwf->ijsf", src_imag, dst_real, precision=highest
    )
    slot_count = source.shape[0]
    merged = jnp.concatenate(
        [
            real_sum.reshape(BLK * BLK, slot_count, NBINS),
            imag_sum.reshape(BLK * BLK, slot_count, NBINS),
        ],
        axis=2,
    )
    return merged * live_slots[None, :, None]


def stack_pairs(partial_value, window_count, wide_count):
    lag_basis = lag_table(NFFT, NBINS, LAGS, window_count)
    slot_count = partial_value.shape[1]
    pair_share = partial_value.shape[0] // wide_count
    summed = lax.psum_scatter(partial_value, "wide", scatter_dimension=0, tiled=True)
    flat = summed.reshape(pair_share * slot_count, 2 * NBINS)
    return jnp.dot(flat, lag_basis, precision=lax.Precision.HIGHEST).reshape(
        pair_share, slot_count, LAGS
    )


def on_device(raw_samples, filter_taps, tile_pairs, tile_owners):
    wide_count = lax.axis_size("wide")
    narrow_count = lax.axis_size("narrow")
    chan_dev = raw_samples.shape[0]
    window_total = raw_samples.shape[1]
    arrived = lax.all_to_all(raw_samples, "wide", split_axis=1, concat_axis=0, tiled=True)
    flat_rows = arrived.reshape(-1, arrived.shape[2])
    whitened = whiten(decimate(flat_rows, filter_taps)).reshape(
        arrived.shape[0], arrived.shape[1], 2 * NBINS
    )
    owner_index = lax.axis_index("narrow")
    slot_ids = jnp.arange(SLOTS, dtype=jnp.int32)
    owner_ids = jnp.arange(narrow_count, dtype=jnp.int32)
    owned_all = tile_owners[None, :] == owner_ids[:, None]
    rank_all = jnp.cumsum(owned_all.astype(jnp.int32), axis=1) - 1
    select_all = owned_all[:, None, :] & (rank_all[:, None, :] == slot_ids[None, :, None])
    select = lax.dynamic_index_in_dim(select_all, owner_index, 0, keepdims=False)
    pick_all = select_all.astype(jnp.int32)
    chosen_all = jnp.sum(pick_all[:, :, :, None] * tile_pairs[None, None, :, :], axis=2)
    chosen = lax.dynamic_index_in_dim(chosen_all, owner_index, 0, keepdims=False)
    live_slots = jnp.sum(select.astype(jnp.int32), axis=1).astype(jnp.float32)
    spectra = lax.all_gather(whitened, "narrow", axis=0, tiled=True)
    source = gather_rows(
        spectra, block_start(chosen[:, 0], chan_dev, wide_count, narrow_count)
    ).astype(jnp.float32)
    target = gather_rows(
        spectra, block_start(chosen[:, 1], chan_dev, wide_count, narrow_count)
    ).astype(jnp.float32)
    partial_value = slot_cross(source, target, live_slots)
    stacked = jnp.transpose(stack_pairs(partial_value, window_total, wide_count), (1, 0, 2))
    return stacked


def solution(mesh):
    in_specs = (P(("wide", "narrow"), None, None), P(), P(), P())
    out_specs = P("narrow", "wide", None)
    return jax.shard_map(
        on_device, mesh=mesh, in_specs=in_specs, out_specs=out_specs, check_vma=False
    )
```

profile of v0, /device:TPU:0, one launch (start us, length us, event | category | flops | bytes accessed | tf_op | source)
XLA Modules:
  0.0 318.2 jit_solution(12943663367902954308)
XLA Ops:
  6.5 4.1 %copy.31 = bf16[8,8,16384]{2,0,1:T(8,128)(2,1)} copy(bf16[8,8,16384]{2,1,0:T(8,128)(2,1)} %param.6) | data formatting | bytes 4194304 | tf_op args[0]
  10.6 5.2 %all-to-all-start = ((bf16[8,8,16384]{2,0,1:T(8,128)(2,1)}), bf16[8,8,16384]{2,0,1:T(8,128)(2,1)S(1)}, u32[]{:S(2)}, u32[]{:S(2)}) async-start(bf16[8,8,16384]{2,0,1:T(8,128)(2,1)} %copy.31), calls=%async_computation | async-start | bytes 4194304 | tf_op jit(solution)/shard_map/all_to_all | solution.py:144
  18.9 69.1 %cosine_convert_fusion = (bf16[4096,1024]{1,0:T(8,128)(2,1)}, bf16[4096,1024]{1,0:T(8,128)(2,1)}) fusion(s32[1024]{0:T(1024)S(1)} %iota_add_fusion), kind=kLoop, calls=%fused_computation.15 | loop fusion | flops 71303168 | bytes 16781312 | tf_op jit(solution)/shard_map/convert.24
  88.1 2.3 reshape_reshape.3
  90.4 43.6 %convolution_bitcast_fusion = f32[2048,128]{0,1:T(8,128)S(1)} fusion(bf16[2048,512]{1,0:T(8,128)(2,1)} %reshape_reshape.3, bf16[]{:T(256)} %bitcast.63, bf16[]{:T(256)} %bitcast.62, bf16[]{:T(256)} %bitcast.61, bf16[]{:T(256)} %bitcast.60, bf16[]{:T(256)} %bitcast.59, bf16[]{:T(256)} %bitcast.58, bf16[]{:T(256)} %bitcast.57, bf16[]{:T(256)} %bitcast.56, ...), kind=kOutput, calls=%fused_computation.33 | convolution fusion | flops 277610496 | bytes 3146368 | tf_op jit(solution)/shard_map/dot_general | solution.py:44
  134.1 41.9 %convolution_bitcast_fusion.1 = f32[2048,128]{0,1:T(8,128)S(1)} fusion(bf16[2048,512]{1,0:T(8,128)(2,1)S(1)} %copy-done.1, bf16[]{:T(256)} %bitcast.63, bf16[]{:T(256)} %bitcast.62, bf16[]{:T(256)} %bitcast.61, bf16[]{:T(256)} %bitcast.60, bf16[]{:T(256)} %bitcast.59, bf16[]{:T(256)} %bitcast.58, bf16[]{:T(256)} %bitcast.57, bf16[]{:T(256)} %bitcast.56, ...), kind=kOutput, calls=%fused_computation.34 | convolution fusion | flops 277544960 | bytes 3146368 | tf_op jit(solution)/shard_map/dot_general | solution.py:41
  176.9 7.6 %fusion.3 = f32[64,2048]{1,0:T(8,128)S(1)} fusion(bf16[4096,1024]{1,0:T(8,128)(2,1)} %get-tuple-element.55, bf16[4096,1024]{1,0:T(8,128)(2,1)} %get-tuple-element.54, bf16[8,8,32,128]{3,2,1,0:T(8,128)(2,1)S(1)} %bitcast.204), kind=kOutput, calls=%fused_computation.10 | convolution fusion | flops 1107296256 | bytes 17825792 | tf_op jit(solution)/shard_map/dot_general | solution.py:77
  184.5 2.4 fusion.585
  188.8 28.9 %all-gather.3.cloned.1.call-done = bf16[256,2048]{1,0:T(8,128)(2,1)} async-done(((bf16[64,2048]{1,0:T(8,128)(2,1)}), bf16[256,2048]{1,0:T(8,128)(2,1)}) %all-gather.3.cloned.1.call-update) | async-done | bytes 1048592 | tf_op jit(solution)/shard_map/all_gather | solution.py:160
  217.6 16.8 %while.2 = (s32[]{:T(128)}, bf16[256,1,2048]{2,0,1:T(8,128)(2,1)}, s32[8,3]{0,1:T(4,128)S(1)}, bf16[8,8,1,2048]{3,1,2,0:T(8,128)(2,1)S(1)}, s32[]{:T(128)}) while((s32[]{:T(128)}, bf16[256,1,2048]{2,0,1:T(8,128)(2,1)}, s32[8,3]{0,1:T(4,128)S(1)}, bf16[8,8,1,2048]{3,1,2,0:T(8,128)(2,1)S(1)}, s32[]{:T(128)}) %tuple.109), condition=%wide.while_cond, body=%wide.while_body.sunk | while | flops 2 | bytes 65641 | solution.py:100
  218.3 1.5 bitcast_dynamic-update-slice_fusion.4
  220.4 1.5 bitcast_dynamic-update-slice_fusion.4
  224.6 1.5 bitcast_dynamic-update-slice_fusion.4
  226.7 1.5 bitcast_dynamic-update-slice_fusion.4
  233.0 1.5 bitcast_dynamic-update-slice_fusion.4
  234.8 16.8 %while.3 = (s32[]{:T(128)}, bf16[256,1,2048]{2,0,1:T(8,128)(2,1)}, s32[8,3]{0,1:T(4,128)S(1)}, bf16[8,8,1,2048]{3,1,2,0:T(8,128)(2,1)S(1)}, s32[]{:T(128)}) while((s32[]{:T(128)}, bf16[256,1,2048]{2,0,1:T(8,128)(2,1)}, s32[8,3]{0,1:T(4,128)S(1)}, bf16[8,8,1,2048]{3,1,2,0:T(8,128)(2,1)S(1)}, s32[]{:T(128)}) %tuple.110), condition=%wide.while_cond.1, body=%wide.while_body.1.sunk | while | flops 2 | bytes 65641 | solution.py:100
  237.6 1.5 bitcast_dynamic-update-slice_fusion.5
  239.7 1.5 bitcast_dynamic-update-slice_fusion.5
  241.8 1.5 bitcast_dynamic-update-slice_fusion.5
  246.0 1.5 bitcast_dynamic-update-slice_fusion.5
  252.6 2.6 maximum_multiply_fusion
  255.2 9.7 %cosine_multiply_fusion = (f32[1024,512]{1,0:T(8,128)S(1)}, f32[1024,512]{1,0:T(8,128)}) fusion(s32[512]{0:T(512)S(1)} %iota_add_fusion.1, s32[1024]{0:T(1024)S(1)} %iota_add_fusion), kind=kLoop, calls=%fused_computation.39 | loop fusion | flops 8912896 | bytes 4200448 | tf_op jit(solution)/shard_map/mul | solution.py:65
  264.9 41.2 %reduce-scatter.2.cloned.1.call-done = f32[8,8,2048]{2,1,0:T(8,128)} async-done(((f32[64,8,2048]{2,1,0:T(8,128)}), f32[8,8,2048]{2,1,0:T(8,128)}) %reduce-scatter.2.cloned.1.call-update) | async-done | bytes 524304 | tf_op jit(solution)/shard_map/reduce_scatter | solution.py:132
  306.2 4.4 %fusion.19 = f32[8,8,512]{2,0,1:T(8,128)S(1)} fusion(f32[8,8,2048]{2,1,0:T(8,128)} %reduce-scatter.2.cloned.1.call-done, f32[1024,512]{1,0:T(8,128)} %get-tuple-element.53, f32[1024,512]{1,0:T(8,128)S(1)} %get-tuple-element.52), kind=kOutput, calls=%fused_computation.44 | convolution fusion | flops 806354944 | bytes 4849664 | tf_op jit(solution)/shard_map/dot_general | solution.py:134
  (87 shorter events, 28.0 us)
Async XLA Ops:
  6.5 9.3 %copy-start = (f32[64]{0:T(128)S(1)}, f32[64]{0:T(128)}, u32[]{:S(2)}) copy-start(f32[64]{0:T(128)} %param.7) | copy-start | bytes 772
  10.6 77.4 %all-to-all-start = ((bf16[8,8,16384]{2,0,1:T(8,128)(2,1)}), bf16[8,8,16384]{2,0,1:T(8,128)(2,1)S(1)}, u32[]{:S(2)}, u32[]{:S(2)}) async-start(bf16[8,8,16384]{2,0,1:T(8,128)(2,1)} %copy.31), calls=%async_computation | async-start | bytes 4194304 | tf_op jit(solution)/shard_map/all_to_all | solution.py:144
  15.8 201.8 %all-gather.3.cloned.1.call-start = ((), (), s32[]{:S(2)}) async-start(), calls=%async_computation.3 | async-start | bytes 1310720 | tf_op jit(solution)/shard_map/all_gather | solution.py:160
  90.4 43.6 %copy-start.1 = (bf16[2048,512]{1,0:T(8,128)(2,1)S(1)}, bf16[2048,512]{1,0:T(8,128)(2,1)}, u32[]{:S(2)}) copy-start(bf16[2048,512]{1,0:T(8,128)(2,1)} %reshape_reshape.3) | copy-start | bytes 6291460
  184.5 3.6 %copy-start.3 = (s32[16]{0:T(128)S(1)}, s32[16]{0:T(128)}, u32[]{:S(2)}) copy-start(s32[16]{0:T(128)} %param.9) | copy-start | bytes 196
  184.5 3.9 %copy-start.2 = (s32[16,2]{0,1:T(2,128)S(1)}, s32[16,2]{0,1:T(2,128)}, u32[]{:S(2)}) copy-start(s32[16,2]{0,1:T(2,128)} %param.8) | copy-start | bytes 388
  187.9 118.3 %reduce-scatter.2.cloned.1.call-start = ((), (), s32[]{:S(2)}) async-start(), calls=%async_computation.2 | async-start | bytes 4718592 | tf_op jit(solution)/shard_map/reduce_scatter | solution.py:132
Sparse Core Ops, SparseCore 0:
  188.0 29.6 all-gather.2
  255.3 50.8 reduce-scatter.1
where the time goes:
time: 320 us; the launch traced here: 318 us
  matrix products  99.9 us (31%)
  other arithmetic  84 us (26%)
  waiting for transfers between devices  70.1 us (22%)
  local copies, waits for them, and re-layouts  44.7 us (14%)
  between operations  13.7 us (4%)
  starting transfers between devices  5.43 us (2%)
    another operation x3, other arithmetic  69.2 us
    dot_general x1, matrix products, decimate(): jnp.dot(segments, last_table, preferred_element_type=jnp.float32)  43.6 us
    dot_general x1, matrix products, decimate(): jnp.dot(segments, this_table, preferred_element_type=jnp.float32)  41.9 us
    reduce_scatter x1, waiting for transfers between devices, stack_pairs(): lax.psum_scatter(partial_value, 'wide', scatter_dimension=0, tiled=True)  41.2 us
    gather x48, local copies, waits for them, and re-layouts  33.3 us
    all_gather x1, waiting for transfers between devices, on_device(): spectra = lax.all_gather(whitened, 'narrow', axis=0, tiled=True)  28.9 us
    mul x1, other arithmetic, lag_table(): jnp.cos(angle) * weight  9.72 us
    dot_general x1, matrix products, whiten(): jnp.dot(decimated, dft_table(decimated.shape[1], NBINS), preferred_elemen...  7.56 us
  transfers between devices with their start and end apart: 3, of which 2 were waited for; matrix products, arithmetic and copies ran while one was open for 26% of the time, Pallas kernels for 0%

commit v1 on v0

v1 whole, which is shorter than its diff:
```python
import math

import jax
import jax.numpy as jnp
import ml_dtypes
import numpy as np
from jax import lax
from jax.sharding import PartitionSpec as P

NFFT = 4096
DECIM = 4
TAPS = 64
NBINS = 1024
HALF = 31
LAGS = 512
BLK = 8
SLOTS = 8
QUARTER = NFFT // 4
SEG = 128
WATER = 0.2
EPS = 1e-06
BF16 = ml_dtypes.bfloat16


def bins_in_order():
    return np.concatenate([np.arange(2, NBINS + 1, 2), np.arange(1, NBINS + 1, 2)])


def dft_tables():
    k = bins_in_order()
    angle = 2.0 * np.pi / NFFT * ((np.arange(QUARTER) + 0.5)[:, None] * k[None, :] % NFFT)
    return np.cos(angle).astype(BF16), (-np.sin(angle)).astype(BF16)


def smoother_tables():
    k = bins_in_order()
    near = np.abs(k[:, None] - k[None, :]) <= HALF
    return near.astype(BF16), (1.0 / near.sum(axis=0)).astype(np.float32)[None, :]


def lag_tables():
    k = bins_in_order()
    lag = np.arange(LAGS) - LAGS // 2
    angle = 2.0 * np.pi / NFFT * (k[:, None] * lag[None, :] % NFFT)
    return np.concatenate([np.cos(angle), -np.sin(angle)], axis=0).astype(BF16)


def fir_table(filter_taps):
    row = jnp.arange(DECIM * SEG + TAPS, dtype=jnp.int32)[:, None]
    col = jnp.arange(SEG, dtype=jnp.int32)[None, :]
    lead = col - row // DECIM + TAPS // DECIM
    by_phase = filter_taps.reshape(TAPS // DECIM, DECIM)[:, ::-1]
    columns = jnp.tile(by_phase.T, (row.shape[0] // DECIM, 1))
    table = jnp.zeros((row.shape[0], SEG), jnp.float32)
    for d in range(TAPS // DECIM):
        table = table + jnp.where(lead == d, columns[:, d : d + 1], 0.0)
    return table.astype(jnp.bfloat16)


def slot_lists(tile_pairs, tile_owners, owners):
    owner_ids = jnp.arange(owners, dtype=jnp.int32)
    slot_ids = jnp.arange(SLOTS, dtype=jnp.int32)
    owned = tile_owners[None, :] == owner_ids[:, None]
    order = jnp.arange(tile_owners.shape[0], dtype=jnp.int32)
    earlier = owned[:, None, :] & (order[None, :, None] > order[None, None, :])
    rank = jnp.sum(earlier.astype(jnp.int32), axis=2)
    pick = (owned[:, None, :] & (rank[:, None, :] == slot_ids[None, :, None])).astype(jnp.int32)
    chosen = jnp.sum(pick[:, :, :, None] * tile_pairs[None, None], axis=2)
    live = jnp.sum(pick, axis=2)
    return chosen.reshape(-1, 2), live.reshape(-1)


def plain_device(raw_samples, filter_taps, tile_pairs, tile_owners):
    wide = lax.axis_size("wide")
    narrow = lax.axis_size("narrow")
    devices = wide * narrow
    mine = NBINS // devices
    chan, windows, length = raw_samples.shape
    rows = chan * windows
    table = fir_table(filter_taps)
    segments = raw_samples.reshape(rows, -1, DECIM * SEG)
    before = jnp.pad(segments[:, :-1, -TAPS:], ((0, 0), (1, 0), (0, 0)))
    quarters = []
    for q in range(4):
        span = slice(q * QUARTER // SEG, (q + 1) * QUARTER // SEG)
        now = table if q % 2 == 0 else table[:, ::-1]
        part = jnp.dot(segments[:, span], now[TAPS:], preferred_element_type=jnp.float32) + jnp.dot(
            before[:, span], now[:TAPS], preferred_element_type=jnp.float32
        )
        if q % 2:
            part = part[:, ::-1]
        quarters.append(part.reshape(rows, QUARTER))
    q0, q1, q2, q3 = quarters
    even, even_back = q0 + q3, q1 + q2
    odd, odd_back = q0 - q3, q1 - q2
    cos_table, sin_table = dft_tables()
    half = NBINS // 2

    def dft(values, part):
        return jnp.dot(values.astype(jnp.bfloat16), part, preferred_element_type=jnp.float32)

    real = jnp.concatenate(
        [dft(even + even_back, cos_table[:, :half]), dft(even - even_back, cos_table[:, half:])], axis=1
    )
    imag = jnp.concatenate(
        [dft(odd - odd_back, sin_table[:, :half]), dft(odd + odd_back, sin_table[:, half:])], axis=1
    )
    near, share = smoother_tables()
    magnitude = jnp.sqrt(real * real + imag * imag)
    smooth = (
        jnp.dot(magnitude.astype(jnp.bfloat16), near, preferred_element_type=jnp.float32) * share
    )
    factor = 1.0 / (smooth + (WATER * jnp.mean(smooth, axis=1, keepdims=True) + EPS))
    white = jnp.stack([real * factor, imag * factor], axis=1).astype(jnp.bfloat16)
    white = white.reshape(chan, windows, 2, devices, mine)
    white = jnp.transpose(white, (3, 0, 1, 2, 4)).reshape(devices, rows, 2 * mine)
    blocks = lax.all_to_all(white, ("wide", "narrow"), split_axis=0, concat_axis=0, tiled=True)
    chosen, live = slot_lists(tile_pairs, tile_owners, narrow)
    block_ids = jnp.arange(devices, dtype=jnp.int32)

    def picked(block, count):
        one_hot = (block[:, None] == block_ids[None, :]) & (count[:, None] > 0)
        rows_of = jnp.dot(
            one_hot.astype(jnp.bfloat16),
            blocks.reshape(devices, -1),
            preferred_element_type=jnp.float32,
        )
        return rows_of.reshape(-1, chan, windows, 2, mine)

    source = picked(chosen[:, 0], live)
    target = picked(chosen[:, 1], live)
    sr, si = source[:, :, None, :, 0], source[:, :, None, :, 1]
    tr, ti = target[:, None, :, :, 0], target[:, None, :, :, 1]
    cross = jnp.stack(
        [jnp.sum(sr * tr + si * ti, axis=3), jnp.sum(sr * ti - si * tr, axis=3)], axis=3
    ).astype(jnp.bfloat16)
    pairs = BLK * BLK // wide
    cross = cross.reshape(narrow, SLOTS, wide, pairs, 2, mine)
    cross = jnp.transpose(cross, (2, 0, 1, 3, 4, 5)).reshape(devices, SLOTS * pairs, 2 * mine)
    got = lax.all_to_all(cross, ("wide", "narrow"), split_axis=0, concat_axis=0, tiled=True)
    got = jnp.transpose(got.reshape(devices, SLOTS * pairs, 2, mine), (1, 2, 0, 3))
    flat = got.reshape(SLOTS * pairs, 2 * NBINS)
    weight = 1.0 / math.sqrt(windows * NBINS)
    stacked = jnp.dot(flat, lag_tables(), preferred_element_type=jnp.float32) * weight
    return stacked.reshape(SLOTS, pairs, LAGS)


def solution(mesh):
    return jax.shard_map(
        plain_device,
        mesh=mesh,
        in_specs=(P(("wide", "narrow"), None, None), P(), P(), P()),
        out_specs=P("narrow", "wide", None),
        check_vma=False,
    )
```

time: 320 us -> 70.3 us (0.22)
  matrix products: 99.9 us -> 8.24 us
  other arithmetic: 84 us -> 12.5 us
  waiting for transfers between devices: 70.1 us -> 9.24 us
  local copies, waits for them, and re-layouts: 44.7 us -> 19.3 us
  between operations: 13.7 us -> 0.5 us
  blocking collectives: 0 us -> 12.7 us
    dot_general x5 -> x16, matrix products: 99.9 us -> 8.24 us  [the longest x2 3.38 us: picked(): jnp.dot(one_hot.astype(jnp.bfloat16), blocks.reshape(devices, -1), prefer...]
    another operation x4 -> x1, other arithmetic: 69.4 us -> 0.12 us
    reduce_scatter x1 -> x0, waiting for transfers between devices: 41.2 us -> none  [stack_pairs(): lax.psum_scatter(partial_value, 'wide', scatter_dimension=0, tiled=True)]
    gather x52 -> x0, local copies, waits for them, and re-layouts: 36.1 us -> none
    all_gather x1 -> x0, waiting for transfers between devices: 28.9 us -> none  [on_device(): spectra = lax.all_gather(whitened, 'narrow', axis=0, tiled=True)]
    all_to_all x0 -> x1, blocking collectives: none -> 12.7 us  [plain_device(): lax.all_to_all(cross, ('wide', 'narrow'), split_axis=0, concat_axis=0, ti...]
    mul x2 -> x0, other arithmetic: 12.3 us -> none  [the longest x1 9.72 us: lag_table(): jnp.cos(angle) * weight]
    all_to_all x1, waiting for transfers between devices: 0.01 us -> 9.24 us  [plain_device(): lax.all_to_all(white, ('wide', 'narrow'), split_axis=0, concat_axis=0, ti...]
  transfers between devices with their start and end apart: 3 -> 1, of which waited for: 2 -> 1; matrix products, arithmetic and copies ran while one was open for 26% -> 1% of each run, Pallas kernels for 0% -> 0%
where the time goes in v1:
time: 70.3 us; the launch traced here: 69.9 us
  local copies, waits for them, and re-layouts  19.3 us (27%)
  blocking collectives  12.7 us (18%)
  other arithmetic  12.5 us (18%)
  waiting for transfers between devices  9.24 us (13%)
  matrix products  8.24 us (12%)
  starting transfers between devices  7.47 us (11%)
    all_to_all x1, blocking collectives, plain_device(): lax.all_to_all(cross, ('wide', 'narrow'), split_axis=0, concat_axis=0, ti...  12.7 us
    all_to_all x1, waiting for transfers between devices, plain_device(): lax.all_to_all(white, ('wide', 'narrow'), split_axis=0, concat_axis=0, ti...  9.24 us
    all_to_all x1, starting transfers between devices, plain_device(): lax.all_to_all(white, ('wide', 'narrow'), split_axis=0, concat_axis=0, ti...  7.47 us
    reduce_sum x1, other arithmetic, plain_device(): jnp.sum(sr * tr + si * ti, axis=3)  7.1 us
    unnamed x29, local copies, waits for them, and re-layouts  4.28 us
    dot_general x2, matrix products, picked(): jnp.dot(one_hot.astype(jnp.bfloat16), blocks.reshape(devices, -1), prefer...  3.38 us
    another operation x4, local copies, waits for them, and re-layouts, plain_device(): jnp.stack([real * factor, imag * factor], axis=1).astype(jnp.bfloat16)  2.93 us
    transpose x1, other arithmetic, plain_device(): jnp.transpose(white, (3, 0, 1, 2, 4)).reshape(devices, rows, 2 * mine)  2.81 us
  transfers between devices with their start and end apart: 1, of which 1 were waited for; matrix products, arithmetic and copies ran while one was open for 1% of the time, Pallas kernels for 0%

profile of v1, /device:TPU:0, one launch (start us, length us, event | category | flops | bytes accessed | tf_op | source)
XLA Modules:
  0.0 69.9 jit_solution(8355193518255798046)
XLA Ops:
  0.0 0.7 %reshape.162 = f32[16,4]{1,0:T(8,128)S(1)} reshape(f32[64]{0:T(128)} %param.12) | data formatting | bytes 512 | tf_op jit(solution)/shard_map/reshape | solution.py:52
  1.0 2.6 %slice_reduce_fusion.15 = (f32[576]{0:T(1024)S(1)}, f32[576]{0:T(1024)S(1)}, f32[576]{0:T(1024)S(1)}, f32[576]{0:T(1024)S(1)}, f32[576]{0:T(1024)S(1)}, /*index=...) fusion(f32[576,16]{1,0:T(8,128)S(1)} %bitcast.105), kind=kLoop, calls=%fused_computation.42 | loop fusion | bytes 73728 | tf_op jit(solution)/shard_map/slice | solution.py:56
  3.6 1.7 %add_convert_fusion = bf16[576,128]{1,0:T(8,128)(2,1)S(1)} fusion(f32[576]{0:T(1024)S(1)} %get-tuple-element.8, f32[576]{0:T(1024)S(1)} %get-tuple-element.9, f32[576]{0:T(1024)S(1)} %get-tuple-element.10, f32[576]{0:T(1024)S(1)} %get-tuple-element.11, f32[576]{0:T(1024)S(1)} %get-tuple-element.12, f32[576]{0:T(1024)S(1)} %get-tuple-element.13, ...), kind=kLoop, calls=%fused_computation.43 | loop fusion | flops 3686400 | bytes 186624 | tf_op jit(solution)/shard_map/convert_element_type | solution.py:57
  5.2 0.8 %copy.106 = bf16[8,8,32,512]{3,2,1,0:T(8,128)(2,1)S(1)} copy(bf16[8,8,32,512]{3,1,2,0:T(8,128)(2,1)S(1)} %bitcast.111) | data formatting | bytes 4194304
  6.7 0.5 slice-done
  11.8 0.6 copy-done.2
  12.4 0.5 fusion.72
  13.5 1.1 %copy.80 = bf16[8,8,1,32,32]{4,2,1,0,3:T(2,128)(2,1)S(1)} copy(bf16[8,8,1,32,32]{4,3,1,0,2:T(8,128)(2,1)S(1)} %stack.18) | data formatting | bytes 262144 | tf_op jit(solution)/shard_map/stack | solution.py:114
  15.0 1.1 %copy.81 = bf16[8,8,1,32,32]{4,2,1,0,3:T(2,128)(2,1)S(1)} copy(bf16[8,8,1,32,32]{4,3,1,0,2:T(8,128)(2,1)S(1)} %stack.19) | data formatting | bytes 262144 | tf_op jit(solution)/shard_map/stack | solution.py:114
  16.1 2.8 %maximum_bitcast_fusion = bf16[32,8,8,2,32]{4,3,2,1,0:T(2,128)(2,1)S(1)} fusion(bf16[8,8,1,32,32]{4,2,1,0,3:T(2,128)(2,1)S(1)} %copy.81, bf16[8,8,1,32,32]{4,2,1,0,3:T(2,128)(2,1)S(1)} %copy.80), kind=kLoop, calls=%fused_computation.17 | loop fusion | flops 524288 | bytes 524288 | tf_op jit(solution)/shard_map/transpose | solution.py:116
  19.4 1.1 %reshape.192 = bf16[32,2,2048]{2,1,0:T(2,128)(2,1)} reshape(bf16[32,64,64]{2,1,0:T(8,128)(2,1)S(1)} %reshape.164) | data formatting | bytes 524288
  20.5 7.5 %all-to-all-start = ((bf16[32,2,2048]{2,1,0:T(2,128)(2,1)}), bf16[32,2,2048]{2,1,0:T(2,128)(2,1)S(1)}, u32[]{:S(2)}, u32[]{:S(2)}) async-start(bf16[32,2,2048]{2,1,0:T(2,128)(2,1)} %reshape.192), calls=%async_computation | async-start | bytes 524288 | tf_op jit(solution)/shard_map/all_to_all | solution.py:117
  28.7 9.2 %all-to-all-done = bf16[32,2,2048]{2,1,0:T(2,128)(2,1)S(1)} async-done(((bf16[32,2,2048]{2,1,0:T(2,128)(2,1)}), bf16[32,2,2048]{2,1,0:T(2,128)(2,1)S(1)}, u32[]{:S(2)}, u32[]{:S(2)}) %all-to-all-start) | async-done | bytes 262176 | tf_op jit(solution)/shard_map/all_to_all | solution.py:117
  38.3 0.8 %copy.94 = bf16[32,64,64]{0,2,1:T(8,128)(2,1)S(1)} copy(bf16[32,64,64]{2,1,0:T(8,128)(2,1)S(1)} %reshape.193) | data formatting | bytes 524288 | tf_op jit(solution)/shard_map/reshape | solution.py:125
  39.1 1.7 %fusion.55 = f32[32,8,8,2,32]{4,0,3,2,1:T(8,128)S(1)} fusion(bf16[8,8,2,32,32]{4,3,2,1,0:T(8,128)(2,1)S(1)} %bitcast.109, s32[32]{0:T(128)S(1)} %get-tuple-element.41, pred[32]{0:T(512)(128)(4,1)S(1)} %gt.34), kind=kOutput, calls=%fused_computation.111 | convolution fusion | flops 8390656 | bytes 786592 | tf_op jit(solution)/shard_map/dot_general | solution.py:123
  41.1 0.6 copy.84
  41.7 1.7 %fusion.51 = f32[32,8,8,2,32]{4,0,3,2,1:T(8,128)S(1)} fusion(bf16[8,8,2,32,32]{4,3,2,1,0:T(8,128)(2,1)S(1)} %bitcast.110, s32[32]{0:T(128)S(1)} %get-tuple-element.40, pred[32]{0:T(512)(128)(4,1)S(1)} %gt.34), kind=kOutput, calls=%fused_computation.108 | convolution fusion | flops 8390656 | bytes 786592 | tf_op jit(solution)/shard_map/dot_general | solution.py:123
  43.6 0.6 copy.83
  44.2 0.6 copy.85
  44.9 0.6 copy.86
  45.5 7.1 %add_reduce_fusion = (bf16[32,8,8,32]{3,2,1,0:T(8,128)(2,1)S(1)}, bf16[32,8,8,32]{3,2,1,0:T(8,128)(2,1)S(1)}) fusion(f32[32,8,8,32]{3,2,1,0:T(8,128)S(1)} %copy.86, f32[32,8,8,32]{3,2,1,0:T(8,128)S(1)} %copy.85, f32[32,8,8,32]{3,2,1,0:T(8,128)S(1)} %copy.84, f32[32,8,8,32]{3,2,1,0:T(8,128)S(1)} %copy.83), kind=kLoop, calls=%fused_computation.1 | loop fusion | flops 4063232 | bytes 1310720 | tf_op jit(solution)/shard_map/reduce_sum | solution.py:135
  52.8 1.6 %copy.87 = bf16[8,4,8,8,2,32]{5,4,3,2,1,0:T(2,128)(2,1)S(1)} copy(bf16[8,4,8,8,2,32]{5,3,0,2,1,4:T(8,128)(2,1)S(1)} %maximum_bitcast_fusion.1) | data formatting | bytes 524288 | tf_op jit(solution)/shard_map/transpose | solution.py:139
  55.4 12.7 %all_to_all.10 = bf16[32,2,2048]{2,1,0:T(2,128)(2,1)S(1)} all-to-all(bf16[32,2,2048]{2,1,0:T(2,128)(2,1)S(1)} %reshape.194), channel_id=1, replica_groups=mesh['wide'=8,'narrow'=4] {'wide','narrow'}, dimensions={0} | all-to-all | bytes 524288 | tf_op jit(solution)/shard_map/all_to_all | solution.py:140
  68.8 1.2 %fusion.3 = f32[8,8,512]{2,1,0:T(8,128)} fusion(bf16[64,2048]{0,1:T(8,128)(2,1)S(1)} %bitcast.115, bf16[2048,512]{1,0:T(8,128)(2,1)S(1)} %copy-done.4), kind=kOutput, calls=%fused_computation.12 | convolution fusion | flops 134250496 | bytes 2490368 | tf_op jit(solution)/shard_map/dot_general | solution.py:144
  (73 shorter events, 10.0 us)
Async XLA Ops:
  1.0 4.3 %copy-start.3 = (bf16[8,8,16384]{2,1,0:T(8,128)(2,1)S(1)}, bf16[8,8,16384]{2,1,0:T(8,128)(2,1)}, u32[]{:S(2)}) copy-start(bf16[8,8,16384]{2,1,0:T(8,128)(2,1)} %param.11) | copy-start | bytes 6291460
  5.2 0.8 %copy-start = (bf16[576,128]{1,0:T(8,128)(2,1)}, bf16[576,128]{1,0:T(8,128)(2,1)S(1)}, u32[]{:S(2)}) copy-start(bf16[576,128]{1,0:T(8,128)(2,1)S(1)} %add_convert_fusion) | copy-start | bytes 442372
  6.5 0.7 %slice-start = ((bf16[576,128]{1,0:T(8,128)(2,1)}), bf16[64,128]{1,0:T(8,128)(2,1)S(1)}, s32[]{:S(2)}) async-start(bf16[576,128]{1,0:T(8,128)(2,1)} %copy-done), calls=%async_computation.2 | async-start | bytes 32768 | tf_op jit(solution)/shard_map/slice | solution.py:88
  6.5 0.9 %slice-start.1 = ((bf16[576,128]{1,0:T(8,128)(2,1)}), bf16[512,128]{1,0:T(8,128)(2,1)S(1)}, s32[]{:S(2)}) async-start(bf16[576,128]{1,0:T(8,128)(2,1)} %copy-done), calls=%async_computation.3 | async-start | bytes 262144 | tf_op jit(solution)/shard_map/slice | solution.py:87
  7.2 1.3 %copy-start.1 = (bf16[576,128]{1,0:T(8,128)(2,1)S(1)}, bf16[576,128]{1,0:T(8,128)(2,1)}, u32[]{:S(2)}) copy-start(bf16[576,128]{1,0:T(8,128)(2,1)} %copy-done) | copy-start | bytes 442372
  9.1 1.2 %copy-start.6 = (bf16[1024,512]{1,0:T(8,128)(2,1)S(1)}, bf16[1024,512]{1,0:T(8,128)(2,1)}, u32[]{:S(2)}) copy-start(bf16[1024,512]{1,0:T(8,128)(2,1)} %constant.79.clone) | copy-start | bytes 3145732
  9.3 1.4 %copy-start.8 = (bf16[1024,512]{1,0:T(8,128)(2,1)S(1)}, bf16[1024,512]{1,0:T(8,128)(2,1)}, u32[]{:S(2)}) copy-start(bf16[1024,512]{1,0:T(8,128)(2,1)} %constant.82.clone) | copy-start | bytes 3145732
  9.7 1.4 %copy-start.7 = (bf16[1024,512]{1,0:T(8,128)(2,1)S(1)}, bf16[1024,512]{1,0:T(8,128)(2,1)}, u32[]{:S(2)}) copy-start(bf16[1024,512]{1,0:T(8,128)(2,1)} %constant.80.clone) | copy-start | bytes 3145732
  9.9 1.5 %copy-start.5 = (bf16[1024,512]{1,0:T(8,128)(2,1)S(1)}, bf16[1024,512]{1,0:T(8,128)(2,1)}, u32[]{:S(2)}) copy-start(bf16[1024,512]{1,0:T(8,128)(2,1)} %constant.81.clone) | copy-start | bytes 3145732
  10.6 1.8 %copy-start.2 = (bf16[1024,1024]{1,0:T(8,128)(2,1)S(1)}, bf16[1024,1024]{1,0:T(8,128)(2,1)}, u32[]{:S(2)}) copy-start(bf16[1024,1024]{1,0:T(8,128)(2,1)} %constant.83.clone) | copy-start | bytes 6291460
  10.7 1.8 %copy-start.9 = (f32[1024]{0:T(1024)S(1)}, f32[1024]{0:T(1024)}, u32[]{:S(2)}) copy-start(f32[1024]{0:T(1024)} %constant.89) | copy-start | bytes 12292
  18.9 9.1 %copy-start.11 = (s32[16]{0:T(128)S(1)}, s32[16]{0:T(128)}, u32[]{:S(2)}) copy-start(s32[16]{0:T(128)} %param.14) | copy-start | bytes 196
  18.9 9.5 %copy-start.10 = (s32[16,2]{0,1:T(2,128)S(1)}, s32[16,2]{0,1:T(2,128)}, u32[]{:S(2)}) copy-start(s32[16,2]{0,1:T(2,128)} %param.13) | copy-start | bytes 388
  20.5 17.5 %all-to-all-start = ((bf16[32,2,2048]{2,1,0:T(2,128)(2,1)}), bf16[32,2,2048]{2,1,0:T(2,128)(2,1)S(1)}, u32[]{:S(2)}, u32[]{:S(2)}) async-start(bf16[32,2,2048]{2,1,0:T(2,128)(2,1)} %reshape.192), calls=%async_computation | async-start | bytes 524288 | tf_op jit(solution)/shard_map/all_to_all | solution.py:117
  55.3 13.4 %copy-start.4 = (bf16[2048,512]{1,0:T(8,128)(2,1)S(1)}, bf16[2048,512]{1,0:T(8,128)(2,1)}, u32[]{:S(2)}) copy-start(bf16[2048,512]{1,0:T(8,128)(2,1)} %constant.85.clone) | copy-start | bytes 6291460

commit v2 on v1

--- a/solution.py
+++ b/solution.py
@@ -1,3 +1,4 @@
+import functools
 import math
 
 import jax
@@ -5,6 +6,8 @@
 import ml_dtypes
 import numpy as np
 from jax import lax
+from jax.experimental import pallas as pl
+from jax.experimental.pallas import tpu as pltpu
 from jax.sharding import PartitionSpec as P
 
 NFFT = 4096
@@ -145,9 +148,291 @@
     return stacked.reshape(SLOTS, pairs, LAGS)
 
 
+WINDOWS = 8
+DEVICES = 32
+LANES = 128
+MINE = NBINS // DEVICES
+ROWS = BLK * WINDOWS
+HALF_ROWS = ROWS // 2
+SPAN = 2 * SEG
+REACH = DECIM * SPAN + LANES
+MESH = pl.DeviceIdType.MESH
+
+
+def row_order():
+    table = np.zeros((ROWS, ROWS), BF16)
+    for window in range(WINDOWS):
+        for chan in range(BLK):
+            table[window * BLK + chan, chan * WINDOWS + window] = 1
+    return table
+
+
+def lane_order():
+    table = np.zeros((4 * LANES, 4 * LANES), BF16)
+    for kind in range(4):
+        for dest in range(4):
+            for b in range(MINE):
+                table[kind * LANES + dest * MINE + b, dest * LANES + kind * MINE + b] = 1
+    return table
+
+
+def paired_lags():
+    real, imag = np.split(lag_tables(), 2)
+    width = 2 * MINE
+    both = np.stack([real.reshape(-1, width, LAGS), imag.reshape(-1, width, LAGS)], axis=1)
+    return both.reshape(2 * NBINS, LAGS)
+
+
+def make_fir(taps, fir):
+    fir[...] = jnp.zeros_like(fir)
+    sub = lax.broadcasted_iota(jnp.int32, (8, LANES), 0)
+    lane = lax.broadcasted_iota(jnp.int32, (8, LANES), 1)
+    for back in range(2):
+        spot = LANES - 1 - lane if back else lane
+        number = DECIM * spot - 1 - sub
+        base = jnp.zeros((8, LANES), jnp.float32)
+        for k in range(TAPS):
+            base = jnp.where(number == k, taps[k], base)
+
+        def row_block(u):
+            shift = 2 * u - 17
+            moved = pltpu.roll(base, (-shift if back else shift) % LANES, 1)
+            at = spot - shift
+            return jnp.where((at >= 0) & (at < 18), moved, 0.0)
+
+        for u in range(0, (DECIM * SEG + TAPS) // 8, 2):
+            rows = jnp.concatenate([row_block(u), row_block(u + 1)], axis=0).astype(jnp.bfloat16)
+            for seg in range(2):
+                top = TAPS + seg * DECIM * SEG + 8 * u
+                left = LANES * (1 - seg if back else seg)
+                fir[back, top : top + 16, left : left + LANES] = rows
+
+
+def local_part(raw, fir, tables, wait, send):
+    cos_table, sin_table, near, share, rows_to, lanes_to = tables
+    quarters = []
+    for q in range(4):
+        parts = []
+        for n in range(4):
+            first = (q * 4 + (3 - n if q % 2 else n)) * DECIM * SPAN
+            if first:
+                parts.append(raw[:, first - LANES : first + DECIM * SPAN])
+            else:
+                parts.append(
+                    jnp.concatenate(
+                        [jnp.zeros((ROWS, LANES), jnp.bfloat16), raw[:, : DECIM * SPAN]], axis=1
+                    )
+                )
+        out = jnp.dot(
+            jnp.concatenate(parts, axis=0), fir[q % 2], preferred_element_type=jnp.float32
+        )
+        quarters.append(
+            jnp.concatenate([out[n * ROWS : (n + 1) * ROWS] for n in range(4)], axis=1)
+        )
+    q0, q1, q2, q3 = quarters
+    even, even_back = q0 + q3, q1 + q2
+    odd, odd_back = q0 - q3, q1 - q2
+    half = NBINS // 2
+
+    def dft(values, part):
+        return jnp.dot(values.astype(jnp.bfloat16), part, preferred_element_type=jnp.float32)
+
+    wait("cos")
+    real = jnp.concatenate(
+        [dft(even + even_back, cos_table[:, :half]), dft(even - even_back, cos_table[:, half:])],
+        axis=1,
+    )
+    wait("sin")
+    imag = jnp.concatenate(
+        [dft(odd - odd_back, sin_table[:, :half]), dft(odd + odd_back, sin_table[:, half:])], axis=1
+    )
+    magnitude = jnp.sqrt(real * real + imag * imag).astype(jnp.bfloat16)
+    wait("near")
+    smooth = jnp.dot(magnitude, near[...], preferred_element_type=jnp.float32) * share[...]
+    factor = 1.0 / (smooth + (WATER * jnp.mean(smooth, axis=1, keepdims=True) + EPS))
+    wait("lanes")
+    real = dft(rows_to[...], (real * factor).astype(jnp.bfloat16)).astype(jnp.bfloat16)
+    imag = dft(rows_to[...], (imag * factor).astype(jnp.bfloat16)).astype(jnp.bfloat16)
+    chunks = []
+    for c in range(NBINS // LANES):
+        cols = slice(c * LANES, (c + 1) * LANES)
+        chunks.append(
+            jnp.concatenate(
+                [
+                    real[:HALF_ROWS, cols],
+                    imag[:HALF_ROWS, cols],
+                    real[HALF_ROWS:, cols],
+                    imag[HALF_ROWS:, cols],
+                ],
+                axis=1,
+            )
+        )
+    moved = jnp.dot(
+        jnp.concatenate(chunks, axis=0), lanes_to[...], preferred_element_type=jnp.float32
+    ).astype(jnp.bfloat16)
+    for p in range(DEVICES):
+        top, left = p // 4 * HALF_ROWS, p % 4 * LANES
+        send[p] = moved[top : top + HALF_ROWS, left : left + LANES]
+
+
+def cross_part(first, second, live, blocks, send):
+    lane = lax.broadcasted_iota(jnp.int32, (BLK, LANES), 1)
+    low = lane % (2 * MINE) < MINE
+    left = lane < LANES // 2
+    lane32 = lax.broadcasted_iota(jnp.int32, (HALF_ROWS, LANES), 1)
+    low32 = lane32 % (2 * MINE) < MINE
+
+    def four_slots(step, _):
+        owner, quad = step // 2, step % 2
+        folded = [[None] * BLK for _ in range(4)]
+        for n in range(4):
+            slot = owner * SLOTS + quad * 4 + n
+            source = blocks[first[slot]].astype(jnp.float32)
+            target = blocks[second[slot]].astype(jnp.float32) * live[slot]
+            turned = jnp.where(
+                low32, pltpu.roll(target, LANES - MINE, 1), -pltpu.roll(target, MINE, 1)
+            )
+            for i in range(BLK):
+                real = imag = None
+                for w in range(4):
+                    one = source[w * BLK + i : w * BLK + i + 1]
+                    r = one * target[w * BLK : (w + 1) * BLK]
+                    m = one * turned[w * BLK : (w + 1) * BLK]
+                    real = r if real is None else real + r
+                    imag = m if imag is None else imag + m
+                both = jnp.where(
+                    left,
+                    real + pltpu.roll(real, LANES // 2, 1),
+                    imag + pltpu.roll(imag, LANES // 2, 1),
+                )
+                folded[n][i] = both + pltpu.roll(both, MINE if n % 2 else LANES - MINE, 1)
+        for i in range(BLK):
+            upper = jnp.where(low, folded[0][i], folded[1][i])
+            lower = jnp.where(low, folded[2][i], folded[3][i])
+            send[i * 4 + owner, pl.ds(pl.multiple_of(quad * 16, 16), 16), :] = jnp.concatenate(
+                [upper, lower], axis=0
+            ).astype(jnp.bfloat16)
+        return 0
+
+    lax.fori_loop(0, 8, four_slots, 0)
+
+
+def lag_part(got, lags, out, weight):
+    lane = lax.broadcasted_iota(jnp.int32, (HALF_ROWS, LANES), 1)
+    low = lane % (2 * MINE) < MINE
+    even, odd = [], []
+    for m in range(DEVICES // 2):
+        one = got[2 * m].astype(jnp.float32)
+        two = got[2 * m + 1].astype(jnp.float32)
+        even.append(jnp.where(low, one, pltpu.roll(two, MINE, 1)))
+        odd.append(jnp.where(low, pltpu.roll(one, LANES - MINE, 1), two))
+    both = jnp.concatenate(
+        [jnp.concatenate(even, axis=1), jnp.concatenate(odd, axis=1)], axis=0
+    ).astype(jnp.bfloat16)
+    result = jnp.dot(both, lags[...], preferred_element_type=jnp.float32) * weight
+    for slot in range(SLOTS):
+        top = slot % 2 * HALF_ROWS + slot // 2 * BLK
+        out[slot] = result[top : top + BLK]
+
+
+def everything(
+    weight, taps, first, second, live, share, raw, cos_h, sin_h, near_h, rows_h, lanes_h, lags_h, out,
+    raw_v, cos_v, sin_v, near_v, rows_v, lanes_v, lags_v, fir, send1, recv1, send2, recv2, load_sems,
+    ssem1, rsem1, ssem2, rsem2,
+):
+    wide, narrow = lax.axis_index("wide"), lax.axis_index("narrow")
+    me = wide * 4 + narrow
+    barrier = pltpu.get_barrier_semaphore()
+
+    def peer(d):
+        p = lax.rem(me + d, DEVICES)
+        return p, (p // 4, lax.rem(p, 4))
+
+    def greet(d, _):
+        pl.semaphore_signal(barrier, inc=1, device_id=peer(d)[1], device_id_type=MESH)
+        return 0
+
+    lax.fori_loop(1, DEVICES, greet, 0)
+    pairs = [(raw, raw_v), (cos_h, cos_v), (sin_h, sin_v), (near_h, near_v), (rows_h, rows_v),
+             (lanes_h, lanes_v), (lags_h, lags_v)]
+    loads = [pltpu.make_async_copy(a, b, load_sems.at[n]) for n, (a, b) in enumerate(pairs)]
+    for load in loads:
+        load.start()
+    make_fir(taps, fir)
+    loads[0].wait()
+
+    def wait(name):
+        for n in {"cos": (1,), "sin": (2,), "near": (3,), "lanes": (4, 5)}[name]:
+            loads[n].wait()
+
+    local_part(raw_v, fir, (cos_v, sin_v, near_v, share, rows_v, lanes_v), wait, send1)
+    pl.semaphore_wait(barrier, DEVICES - 1)
+
+    def exchange(send, recv, ssem, rsem):
+        def start(d, _):
+            p, where = peer(d)
+            pltpu.make_async_remote_copy(
+                src_ref=send.at[p], dst_ref=recv.at[me], send_sem=ssem.at[p], recv_sem=rsem.at[me],
+                device_id=where, device_id_type=MESH,
+            ).start()
+            return 0
+
+        def finish(d, _):
+            p, where = peer(d)
+            pltpu.make_async_remote_copy(
+                src_ref=send.at[p], dst_ref=recv.at[p], send_sem=ssem.at[p], recv_sem=rsem.at[p],
+                device_id=where, device_id_type=MESH,
+            ).wait()
+            return 0
+
+        lax.fori_loop(1, DEVICES, start, 0)
+        recv[me] = send[me]
+        lax.fori_loop(1, DEVICES, finish, 0)
+
+    exchange(send1, recv1, ssem1, rsem1)
+    cross_part(first, second, live, recv1, send2)
+    exchange(send2, recv2, ssem2, rsem2)
+    loads[6].wait()
+    lag_part(recv2, lags_v, out, weight)
+
+
+def fused_device(raw_samples, filter_taps, tile_pairs, tile_owners):
+    raw = raw_samples.reshape(ROWS, -1)
+    chosen, live = slot_lists(tile_pairs, tile_owners, 4)
+    cos_table, sin_table = dft_tables()
+    near, share = smoother_tables()
+    held = [raw, cos_table, sin_table, near, row_order(), lane_order(), paired_lags()]
+    smem = pl.BlockSpec(memory_space=pltpu.SMEM)
+    vmem = pl.BlockSpec(memory_space=pltpu.VMEM)
+    exchanged = pltpu.VMEM((DEVICES, HALF_ROWS, LANES), jnp.bfloat16)
+    return pl.pallas_call(
+        functools.partial(everything, 1.0 / math.sqrt(WINDOWS * NBINS)),
+        out_shape=jax.ShapeDtypeStruct((SLOTS, BLK, LAGS), jnp.float32),
+        in_specs=[smem] * 4 + [vmem] + [pl.BlockSpec(memory_space=pl.ANY)] * len(held),
+        out_specs=vmem,
+        scratch_shapes=[pltpu.VMEM(a.shape, jnp.bfloat16) for a in held]
+        + [pltpu.VMEM((2, REACH, SPAN), jnp.bfloat16)]
+        + [exchanged] * 4
+        + [pltpu.SemaphoreType.DMA((len(held),))]
+        + [pltpu.SemaphoreType.DMA((DEVICES,))] * 4,
+        compiler_params=pltpu.CompilerParams(
+            collective_id=0, has_side_effects=True, vmem_limit_bytes=50 * 2**20
+        ),
+    )(
+        filter_taps, chosen[:, 0], chosen[:, 1], live.astype(jnp.float32), jnp.asarray(share),
+        *(jnp.asarray(a) for a in held),
+    )
+
+
 def solution(mesh):
+    fits = mesh.shape["wide"] == BLK and mesh.shape["narrow"] == 4
+
+    def on_device(raw_samples, *rest):
+        kept = fits and raw_samples.shape[:2] == (BLK, WINDOWS)
+        return (fused_device if kept else plain_device)(raw_samples, *rest)
+
     return jax.shard_map(
-        plain_device,
+        on_device,
         mesh=mesh,
         in_specs=(P(("wide", "narrow"), None, None), P(), P(), P()),
         out_specs=P("narrow", "wide", None),

time: 70.3 us -> 36.4 us (0.52)
  Pallas kernels: 0 us -> 28.6 us
  local copies, waits for them, and re-layouts: 19.3 us -> 5.53 us
  blocking collectives: 12.7 us -> 0 us
  other arithmetic: 12.5 us -> 1.87 us
  waiting for transfers between devices: 9.24 us -> 0 us
  matrix products: 8.24 us -> 0 us
  starting transfers between devices: 7.47 us -> 0 us
    pallas_call x0 -> x1, Pallas kernels: none -> 28.6 us  [fused_device(): pl.pallas_call(functools.partial(everything, 1.0 / math.sqrt(WINDOWS * NB...]
    all_to_all x1 -> x0, blocking collectives: 12.7 us -> none  [plain_device(): lax.all_to_all(cross, ('wide', 'narrow'), split_axis=0, concat_axis=0, ti...]
    all_to_all x1 -> x0, waiting for transfers between devices: 9.24 us -> none  [plain_device(): lax.all_to_all(white, ('wide', 'narrow'), split_axis=0, concat_axis=0, ti...]
    dot_general x16 -> x0, matrix products: 8.24 us -> none  [the longest x2 3.38 us: picked(): jnp.dot(one_hot.astype(jnp.bfloat16), blocks.reshape(devices, -1), prefer...]
    all_to_all x1 -> x0, starting transfers between devices: 7.47 us -> none  [plain_device(): lax.all_to_all(white, ('wide', 'narrow'), split_axis=0, concat_axis=0, ti...]
    reduce_sum x1 -> x0, other arithmetic: 7.1 us -> none  [plain_device(): jnp.sum(sr * tr + si * ti, axis=3)]
    slice x11 -> x0, local copies, waits for them, and re-layouts: 4.33 us -> none  [the longest x1 2.58 us: fir_table(): table = table + jnp.where(lead == d, columns[:, d:d + 1], 0.0)]
    transpose x2 -> x0, other arithmetic: 3.04 us -> none  [the longest x1 2.81 us: plain_device(): jnp.transpose(white, (3, 0, 1, 2, 4)).reshape(devices, rows, 2 * mine)]
  transfers between devices with their start and end apart: 1 -> 0, of which waited for: 1 -> 0; matrix products, arithmetic and copies ran while one was open for 1% -> 0% of each run, Pallas kernels for 0% -> 0%
where the time goes in v2:
time: 36.4 us; the launch traced here: 36.1 us
  Pallas kernels  28.6 us (79%)
  local copies, waits for them, and re-layouts  5.53 us (15%)
  other arithmetic  1.87 us (5%)
    pallas_call x1, Pallas kernels, fused_device(): pl.pallas_call(functools.partial(everything, 1.0 / math.sqrt(WINDOWS * NB...  28.6 us
    unnamed x11, local copies, waits for them, and re-layouts  5.35 us
    reduce_sum x1, other arithmetic, slot_lists(): chosen = jnp.sum(pick[:, :, :, None] * tile_pairs[None, None], axis=2)  0.89 us

profile of v2, /device:TPU:0, one launch (start us, length us, event | category | flops | bytes accessed | tf_op | source)
XLA Modules:
  0.0 36.1 jit_solution(258334627549094726)
XLA Ops:
  0.0 0.7 %iota_compare_fusion.2 = pred[4,16]{1,0:T(4,128)(4,1)S(1)} fusion(s32[16]{0:T(128)} %param.14), kind=kLoop, calls=%fused_computation.7 | loop fusion | flops 64 | bytes 128 | tf_op jit(solution)/shard_map/eq | solution.py:66
  0.7 0.1 convert_reduce_fusion
  0.8 0.1 fusion.2
  1.0 0.1 convert_element_type.18.live
  1.1 0.9 %multiply_reduce_fusion = s32[4,8,2]{1,2,0:T(2,128)S(1)} fusion(s32[16,2]{0,1:T(2,128)} %param.13, s32[4,8,16]{2,1,0:T(8,128)S(1)} %fusion.1), kind=kLoop, calls=%fused_computation | loop fusion | flops 1984 | bytes 2432 | tf_op jit(solution)/shard_map/reduce_sum | solution.py:71
  2.0 0.1 reshape.47
  2.1 0.0 copy-start
  2.1 1.6 %copy-done = bf16[8,8,16384]{2,1,0:T(8,128)(2,1)S(1)} copy-done((bf16[8,8,16384]{2,1,0:T(8,128)(2,1)S(1)}, bf16[8,8,16384]{2,1,0:T(8,128)(2,1)}, u32[]{:S(2)}) %copy-start) | copy-done | bytes 2097176
  3.7 0.0 copy-start.1
  3.7 1.0 %copy-done.1 = bf16[512,512]{1,0:T(8,128)(2,1)S(1)} copy-done((bf16[512,512]{1,0:T(8,128)(2,1)S(1)}, bf16[512,512]{1,0:T(8,128)(2,1)}, u32[]{:S(2)}) %copy-start.1) | copy-done | bytes 524312
  4.7 0.0 copy-start.2
  4.7 0.7 %copy-done.2 = bf16[64,64]{1,0:T(8,128)(2,1)S(1)} copy-done((bf16[64,64]{1,0:T(8,128)(2,1)S(1)}, bf16[64,64]{1,0:T(8,128)(2,1)}, u32[]{:S(2)}) %copy-start.2) | copy-done | bytes 8216
  5.4 0.0 copy-start.3
  5.4 0.7 %copy-done.3 = f32[1,1024]{1,0:T(1,128)S(1)} copy-done((f32[1,1024]{1,0:T(1,128)S(1)}, f32[1,1024]{1,0:T(1,128)}, u32[]{:S(2)}) %copy-start.3) | copy-done | bytes 4120
  6.1 0.0 copy-start.4
  6.1 0.7 %copy-done.4 = f32[64]{0:T(128)S(1)} copy-done((f32[64]{0:T(128)S(1)}, f32[64]{0:T(128)}, u32[]{:S(2)}) %copy-start.4) | copy-done | bytes 280
  6.8 28.6 %shard_map.109 = f32[8,8,512]{2,1,0:T(8,128)S(1)} custom-call(f32[64]{0:T(128)S(1)} %copy-done.4, s32[32]{0:T(128)S(1)} %get-tuple-element.6.first, s32[32]{0:T(128)S(1)} %get-tuple-element.5.second, f32[32]{0:T(128)S(1)} %convert_element_type.18.live, f32[1,1024]{1,0:T(1,128)S(1)} %copy-done.3, bf16[64,16384]{1,0:T(8,128)(2,1)S(1)} %bitcast.7, ...), custom_call_target="tpu_custom_call" | custom-call | tf_op jit(solution)/shard_map/pallas_call | solution.py:408
  35.4 0.7 %copy.15 = f32[8,8,512]{2,1,0:T(8,128)} copy(f32[8,8,512]{2,1,0:T(8,128)S(1)} %shard_map.109) | data formatting | bytes 262144
  (5 shorter events, 0.0 us)
Async XLA Ops:
  2.1 1.6 %copy-start = (bf16[8,8,16384]{2,1,0:T(8,128)(2,1)S(1)}, bf16[8,8,16384]{2,1,0:T(8,128)(2,1)}, u32[]{:S(2)}) copy-start(bf16[8,8,16384]{2,1,0:T(8,128)(2,1)} %param.11) | copy-start | bytes 6291460
  3.7 1.0 %copy-start.1 = (bf16[512,512]{1,0:T(8,128)(2,1)S(1)}, bf16[512,512]{1,0:T(8,128)(2,1)}, u32[]{:S(2)}) copy-start(bf16[512,512]{1,0:T(8,128)(2,1)} %constant.21.clone.lanes_h) | copy-start | bytes 1572868
  4.7 0.7 %copy-start.2 = (bf16[64,64]{1,0:T(8,128)(2,1)S(1)}, bf16[64,64]{1,0:T(8,128)(2,1)}, u32[]{:S(2)}) copy-start(bf16[64,64]{1,0:T(8,128)(2,1)} %constant.20.clone.rows_h) | copy-start | bytes 24580
  5.4 0.7 %copy-start.3 = (f32[1,1024]{1,0:T(1,128)S(1)}, f32[1,1024]{1,0:T(1,128)}, u32[]{:S(2)}) copy-start(f32[1,1024]{1,0:T(1,128)} %constant.16.clone.share) | copy-start | bytes 12292
  6.1 0.7 %copy-start.4 = (f32[64]{0:T(128)S(1)}, f32[64]{0:T(128)}, u32[]{:S(2)}) copy-start(f32[64]{0:T(128)} %taps.1) | copy-start | bytes 772

commit v3 on v2

--- a/solution.py
+++ b/solution.py
@@ -275,15 +275,33 @@
         send[p] = moved[top : top + HALF_ROWS, left : left + LANES]
 
 
-def cross_part(first, second, live, blocks, send):
+def list_slots(pairs, owners, first, second, live):
+    def one_slot(slot, _):
+        owner, rank = slot // SLOTS, slot % SLOTS
+        count = a = b = held = jnp.int32(0)
+        for t in range(owners.shape[0]):
+            mine = owners[t] == owner
+            hit = mine & (count == rank)
+            a = jnp.where(hit, pairs[t, 0], a)
+            b = jnp.where(hit, pairs[t, 1], b)
+            held = jnp.where(hit, 1, held)
+            count = jnp.where(mine, count + 1, count)
+        first[slot] = a
+        second[slot] = b
+        live[slot] = held.astype(jnp.float32)
+        return 0
+
+    lax.fori_loop(0, 4 * SLOTS, one_slot, 0)
+
+
+def cross_part(first, second, live, blocks, send, owner_at, sent):
     lane = lax.broadcasted_iota(jnp.int32, (BLK, LANES), 1)
     low = lane % (2 * MINE) < MINE
     left = lane < LANES // 2
     lane32 = lax.broadcasted_iota(jnp.int32, (HALF_ROWS, LANES), 1)
     low32 = lane32 % (2 * MINE) < MINE
 
-    def four_slots(step, _):
-        owner, quad = step // 2, step % 2
+    def four_slots(owner, quad):
         folded = [[None] * BLK for _ in range(4)]
         for n in range(4):
             slot = owner * SLOTS + quad * 4 + n
@@ -312,9 +330,19 @@
             send[i * 4 + owner, pl.ds(pl.multiple_of(quad * 16, 16), 16), :] = jnp.concatenate(
                 [upper, lower], axis=0
             ).astype(jnp.bfloat16)
-        return 0
-
-    lax.fori_loop(0, 8, four_slots, 0)
+
+    def one_owner(k, _):
+        owner = owner_at(k)
+
+        def half(quad, _):
+            four_slots(owner, quad)
+            return 0
+
+        lax.fori_loop(0, 2, half, 0)
+        sent(k)
+        return 0
+
+    lax.fori_loop(0, 4, one_owner, 0)
 
 
 def lag_part(got, lags, out, weight):
@@ -336,23 +364,26 @@
 
 
 def everything(
-    weight, taps, first, second, live, share, raw, cos_h, sin_h, near_h, rows_h, lanes_h, lags_h, out,
+    weight, taps, pairs_s, owners_s, share, raw, cos_h, sin_h, near_h, rows_h, lanes_h, lags_h, out,
     raw_v, cos_v, sin_v, near_v, rows_v, lanes_v, lags_v, fir, send1, recv1, send2, recv2, load_sems,
-    ssem1, rsem1, ssem2, rsem2,
+    ssem1, rsem1, ssem2, rsem2, first, second, live,
 ):
     wide, narrow = lax.axis_index("wide"), lax.axis_index("narrow")
     me = wide * 4 + narrow
     barrier = pltpu.get_barrier_semaphore()
 
+    def owner_at(k):
+        return lax.rem(narrow + 1 + k, 4)
+
     def peer(d):
-        p = lax.rem(me + d, DEVICES)
-        return p, (p // 4, lax.rem(p, 4))
+        to = (lax.rem(wide + lax.rem(d + 1, 8), 8), owner_at(d // 8))
+        return to[0] * 4 + to[1], to
 
     def greet(d, _):
         pl.semaphore_signal(barrier, inc=1, device_id=peer(d)[1], device_id_type=MESH)
         return 0
 
-    lax.fori_loop(1, DEVICES, greet, 0)
+    lax.fori_loop(0, DEVICES - 1, greet, 0)
     pairs = [(raw, raw_v), (cos_h, cos_v), (sin_h, sin_v), (near_h, near_v), (rows_h, rows_v),
              (lanes_h, lanes_v), (lags_h, lags_v)]
     loads = [pltpu.make_async_copy(a, b, load_sems.at[n]) for n, (a, b) in enumerate(pairs)]
@@ -368,37 +399,48 @@
     local_part(raw_v, fir, (cos_v, sin_v, near_v, share, rows_v, lanes_v), wait, send1)
     pl.semaphore_wait(barrier, DEVICES - 1)
 
-    def exchange(send, recv, ssem, rsem):
-        def start(d, _):
-            p, where = peer(d)
-            pltpu.make_async_remote_copy(
-                src_ref=send.at[p], dst_ref=recv.at[me], send_sem=ssem.at[p], recv_sem=rsem.at[me],
-                device_id=where, device_id_type=MESH,
-            ).start()
+    def copy(d, send, recv, ssem, rsem, at):
+        p, where = peer(d)
+        at = p if at is None else at
+        return pltpu.make_async_remote_copy(
+            src_ref=send.at[p], dst_ref=recv.at[at], send_sem=ssem.at[p], recv_sem=rsem.at[at],
+            device_id=where, device_id_type=MESH,
+        )
+
+    one, two = (send1, recv1, ssem1, rsem1), (send2, recv2, ssem2, rsem2)
+
+    def start1(d, _):
+        copy(d, *one, me).start()
+        return 0
+
+    def finish1(d, _):
+        copy(d, *one, None).wait()
+        return 0
+
+    def finish2(d, _):
+        copy(d, *two, None).wait()
+        return 0
+
+    def sent(k):
+        def start2(d, _):
+            copy(d, *two, me).start()
             return 0
 
-        def finish(d, _):
-            p, where = peer(d)
-            pltpu.make_async_remote_copy(
-                src_ref=send.at[p], dst_ref=recv.at[p], send_sem=ssem.at[p], recv_sem=rsem.at[p],
-                device_id=where, device_id_type=MESH,
-            ).wait()
-            return 0
-
-        lax.fori_loop(1, DEVICES, start, 0)
-        recv[me] = send[me]
-        lax.fori_loop(1, DEVICES, finish, 0)
-
-    exchange(send1, recv1, ssem1, rsem1)
-    cross_part(first, second, live, recv1, send2)
-    exchange(send2, recv2, ssem2, rsem2)
+        lax.fori_loop(k * 8, jnp.minimum(k * 8 + 8, DEVICES - 1), start2, 0)
+
+    lax.fori_loop(0, DEVICES - 1, start1, 0)
+    recv1[me] = send1[me]
+    list_slots(pairs_s, owners_s, first, second, live)
+    lax.fori_loop(0, DEVICES - 1, finish1, 0)
+    cross_part(first, second, live, recv1, send2, owner_at, sent)
+    recv2[me] = send2[me]
+    lax.fori_loop(0, DEVICES - 1, finish2, 0)
     loads[6].wait()
     lag_part(recv2, lags_v, out, weight)
 
 
 def fused_device(raw_samples, filter_taps, tile_pairs, tile_owners):
     raw = raw_samples.reshape(ROWS, -1)
-    chosen, live = slot_lists(tile_pairs, tile_owners, 4)
     cos_table, sin_table = dft_tables()
     near, share = smoother_tables()
     held = [raw, cos_table, sin_table, near, row_order(), lane_order(), paired_lags()]
@@ -408,18 +450,19 @@
     return pl.pallas_call(
         functools.partial(everything, 1.0 / math.sqrt(WINDOWS * NBINS)),
         out_shape=jax.ShapeDtypeStruct((SLOTS, BLK, LAGS), jnp.float32),
-        in_specs=[smem] * 4 + [vmem] + [pl.BlockSpec(memory_space=pl.ANY)] * len(held),
+        in_specs=[smem] * 3 + [vmem] + [pl.BlockSpec(memory_space=pl.ANY)] * len(held),
         out_specs=vmem,
         scratch_shapes=[pltpu.VMEM(a.shape, jnp.bfloat16) for a in held]
         + [pltpu.VMEM((2, REACH, SPAN), jnp.bfloat16)]
         + [exchanged] * 4
         + [pltpu.SemaphoreType.DMA((len(held),))]
-        + [pltpu.SemaphoreType.DMA((DEVICES,))] * 4,
+        + [pltpu.SemaphoreType.DMA((DEVICES,))] * 4
+        + [pltpu.SMEM((4 * SLOTS,), kind) for kind in (jnp.int32, jnp.int32, jnp.float32)],
         compiler_params=pltpu.CompilerParams(
-            collective_id=0, has_side_effects=True, vmem_limit_bytes=50 * 2**20
+            collective_id=0, has_side_effects=True, vmem_limit_bytes=60 * 2**20
         ),
     )(
-        filter_taps, chosen[:, 0], chosen[:, 1], live.astype(jnp.float32), jnp.asarray(share),
+        filter_taps, tile_pairs, tile_owners, jnp.asarray(share),
         *(jnp.asarray(a) for a in held),
     )
 

time: 36.4 us -> 31.2 us (0.86)
  local copies, waits for them, and re-layouts: 5.53 us -> 2.92 us
  other arithmetic: 1.87 us -> 0 us
  Pallas kernels: 28.6 us -> 28.1 us
    unnamed x11 -> x2, local copies, waits for them, and re-layouts: 5.35 us -> 2.92 us
    reduce_sum x3 -> x0, other arithmetic: 1.19 us -> none  [the longest x1 0.89 us: slot_lists(): chosen = jnp.sum(pick[:, :, :, None] * tile_pairs[None, None], axis=2)]
    eq x1 -> x0, other arithmetic: 0.66 us -> none  [slot_lists(): owned = tile_owners[None, :] == owner_ids[:, None]]
    pallas_call x1, Pallas kernels: 28.6 us -> 28.1 us  [fused_device(): pl.pallas_call(functools.partial(everything, 1.0 / math.sqrt(WINDOWS * NB...]
where the time goes in v3:
time: 31.2 us; the launch traced here: 31.1 us
  Pallas kernels  28.1 us (90%)
  local copies, waits for them, and re-layouts  2.92 us (9%)
    pallas_call x1, Pallas kernels, fused_device(): pl.pallas_call(functools.partial(everything, 1.0 / math.sqrt(WINDOWS * NB...  28.1 us
    unnamed x2, local copies, waits for them, and re-layouts  2.92 us

profile of v3, /device:TPU:0, one launch (start us, length us, event | category | flops | bytes accessed | tf_op | source)
XLA Modules:
  0.0 31.1 jit_solution(4818582688265363100)
XLA Ops:
  0.0 1.4 %copy.12.pairs_s = s32[16,2]{1,0:T(8,128)} copy(s32[16,2]{0,1:T(2,128)} %param.13) | data formatting | bytes 256 | tf_op args[2]
  1.4 28.1 %shard_map.109 = f32[8,8,512]{2,1,0:T(8,128)} custom-call(f32[64]{0:T(128)} %taps.1, s32[16,2]{1,0:T(8,128)} %copy.12.pairs_s, s32[16]{0:T(128)} %owners_s.1, f32[1,1024]{1,0:T(1,128)} %constant.14.clone.share, bf16[64,16384]{1,0:T(8,128)(2,1)} %bitcast.1, bf16[1024,1024]{1,0:T(8,128)(2,1)} %constant.15.clone.cos_h, ...), custom_call_target="tpu_custom_call" | custom-call | tf_op jit(solution)/shard_map/pallas_call | solution.py:450
  29.5 1.6 %copy.14 = f32[8,8,512]{2,1,0:T(8,128)} copy(f32[8,8,512]{2,1,0:T(8,128)} %shard_map.109) | data formatting | bytes 262144

commit v4 on v3

--- a/solution.py
+++ b/solution.py
@@ -383,12 +383,12 @@
         pl.semaphore_signal(barrier, inc=1, device_id=peer(d)[1], device_id_type=MESH)
         return 0
 
-    lax.fori_loop(0, DEVICES - 1, greet, 0)
     pairs = [(raw, raw_v), (cos_h, cos_v), (sin_h, sin_v), (near_h, near_v), (rows_h, rows_v),
              (lanes_h, lanes_v), (lags_h, lags_v)]
     loads = [pltpu.make_async_copy(a, b, load_sems.at[n]) for n, (a, b) in enumerate(pairs)]
     for load in loads:
         load.start()
+    lax.fori_loop(0, DEVICES - 1, greet, 0)
     make_fir(taps, fir)
     loads[0].wait()
 

time: 31.2 us -> 30.4 us (0.974)
  Pallas kernels: 28.1 us -> 27.3 us
    pallas_call x1, Pallas kernels: 28.1 us -> 27.3 us  [fused_device(): pl.pallas_call(functools.partial(everything, 1.0 / math.sqrt(WINDOWS * NB...]
where the time goes in v4:
time: 30.4 us; the launch traced here: 30.2 us
  Pallas kernels  27.3 us (90%)
  local copies, waits for them, and re-layouts  2.92 us (10%)
    pallas_call x1, Pallas kernels, fused_device(): pl.pallas_call(functools.partial(everything, 1.0 / math.sqrt(WINDOWS * NB...  27.3 us
    unnamed x2, local copies, waits for them, and re-layouts  2.92 us

profile of v4, /device:TPU:0, one launch (start us, length us, event | category | flops | bytes accessed | tf_op | source)
XLA Modules:
  0.0 30.2 jit_solution(2876181426890052801)
XLA Ops:
  0.0 1.4 %copy.12.pairs_s = s32[16,2]{1,0:T(8,128)} copy(s32[16,2]{0,1:T(2,128)} %param.13) | data formatting | bytes 256 | tf_op args[2]
  1.4 27.3 %shard_map.109 = f32[8,8,512]{2,1,0:T(8,128)} custom-call(f32[64]{0:T(128)} %taps.1, s32[16,2]{1,0:T(8,128)} %copy.12.pairs_s, s32[16]{0:T(128)} %owners_s.1, f32[1,1024]{1,0:T(1,128)} %constant.14.clone.share, bf16[64,16384]{1,0:T(8,128)(2,1)} %bitcast.1, bf16[1024,1024]{1,0:T(8,128)(2,1)} %constant.15.clone.cos_h, ...), custom_call_target="tpu_custom_call" | custom-call | tf_op jit(solution)/shard_map/pallas_call | solution.py:450
  28.6 1.6 %copy.14 = f32[8,8,512]{2,1,0:T(8,128)} copy(f32[8,8,512]{2,1,0:T(8,128)} %shard_map.109) | data formatting | bytes 262144
